TPU v7x, 32 devices: a whole 2x2x4 slice. The times are simulated.
32 devices in a mesh: seq: 8 (over z, core), head: 4 (over y, x).
Axes of the slice: x: 2, y: 2, z: 4, core: 2. Of those that a mesh axis runs over, the one named last changes fastest.
Arguments:
- queries: bfloat16 [2048, 8192], P('seq', 'head'), may hold values from -6 to 6
- key_input: bfloat16 [2048, 8192], P('seq', 'head'), may hold values from -6 to 6
- value_input: bfloat16 [2048, 8192], P('seq', 'head'), may hold values from -6 to 6
- out_gate: bfloat16 [2048, 8192], P('seq', 'head'), may hold values from -8 to 8
- log_decay: float32 [64, 2048], P('head', 'seq'), may hold values from -1 to 0, as said below
- norm_gain: float32 [8192], P('head'), may hold values from 0.1 to 1.9
- features: bfloat16 [2048, 6144], P('seq', 'head'), may hold values from -6 to 6
- expert_ids: int32 [2048, 2], P('seq'), may hold values from 0 to 31, as said below
- route_weight: float32 [2048, 2], P('seq'), may hold values from 0.25 to 1
- placement: int32 [4], replicated, may hold values from 0 to 31, as said below
- gate_weight: bfloat16 [6144, 36864], P('head', 'seq'), may hold values from -0.078125 to 0.078125
- up_weight: bfloat16 [6144, 36864], P('head', 'seq'), may hold values from -0.078125 to 0.078125
- down_weight: bfloat16 [36864, 6144], P('seq', 'head'), may hold values from -0.0625 to 0.0625
Outputs:
- attention_out: bfloat16 [2048, 8192], P('seq', 'head')
- moe_out: bfloat16 [2048, 6144], P('seq', 'head')
Inputs may be any that keep to these rules, and one draw needn't show every extreme that they name: `expert_ids`: in each aligned block of 256 tokens, each expert named in placement is named by at most 8 tokens, and the same one of them by exactly 8 tokens in every block; the two ids of a token differ. `placement`: 4 different expert numbers, among them always 0 and 31. `log_decay`: every entry is negative.
All inputs are finite; a program needn't handle non-finite values.
Results may differ from a plain program's by a relative error of at most 0.0058.
Values may be sent and summed in bfloat16 or wider, within the bound.
A program may use at most 128 MiB of HBM per device.

v0:
```python
import jax
import jax.numpy as jnp
from jax import lax
from jax.sharding import PartitionSpec as P

EXP_FLY = 4
CAP = 8


norm_eps = 1e-06


def prefix(part, axis, combine, identity):
    place = lax.axis_index(axis)
    gathered = jax.tree.map(lambda a: lax.all_gather(a, axis), part)
    state = jax.tree.map(lambda a, e: jnp.zeros_like(a) + jnp.asarray(e, a.dtype), part, identity)

    def one(step, state):
        return combine(
            state, jax.tree.map(lambda a: lax.dynamic_index_in_dim(a, step, 0, False), gathered)
        )

    return lax.fori_loop(0, place, one, state)


def slot_table(pairs, placement, slots):
    flat = pairs.reshape(-1)
    match = (flat[:, None] == placement[None, :]).astype(jnp.int32)
    rank = jnp.cumsum(match, axis=0) - 1
    order = jnp.arange(slots, dtype=jnp.int32)
    hits = (match[None, :, :] == 1) & (rank[None, :, :] == order[:, None, None])
    return jnp.transpose(hits, (2, 0, 1))


def combine_states(earlier, later):
    return (earlier[0] * later[0], later[0][:, None, None] * earlier[1] + later[1])


def per_device(
    queries,
    key_input,
    value_input,
    out_gate,
    log_decay,
    norm_gain,
    features,
    expert_ids,
    route_weight,
    placement,
    gate_weight,
    up_weight,
    down_weight,
):
    tokens = queries.shape[0]
    heads_here = log_decay.shape[0]
    width = queries.shape[1] // heads_here
    query_h = queries.reshape(tokens, heads_here, width)
    key_h = key_input.reshape(tokens, heads_here, width)
    value_h = value_input.reshape(tokens, heads_here, width)
    decay_sum = jnp.cumsum(log_decay, axis=1)
    last = decay_sum[:, -1]
    key_scaled = key_h.astype(jnp.float32) * jnp.exp(last[:, None] - decay_sum).T[:, :, None]
    local_state = jnp.einsum(
        "thd,the->hde", key_scaled, value_h.astype(jnp.float32), precision=lax.Precision.HIGHEST
    )
    ones = jnp.ones_like(last)
    zeros = jnp.zeros_like(local_state)
    moved = prefix((jnp.exp(last), local_state), "seq", combine_states, (ones, zeros))
    state_in = moved[1]
    scores = jnp.einsum("thd,shd->hts", query_h, key_h, preferred_element_type=jnp.float32)
    lower = jnp.arange(tokens)[:, None] >= jnp.arange(tokens)[None, :]
    spread = decay_sum[:, :, None] - decay_sum[:, None, :]
    weights = jnp.exp(jnp.where(lower[None], spread, -jnp.inf))
    probs = (scores * weights).astype(jnp.bfloat16)
    intra = jnp.einsum("hts,shd->thd", probs, value_h, preferred_element_type=jnp.float32)
    query_scaled = query_h.astype(jnp.float32) * jnp.exp(decay_sum).T[:, :, None]
    inter = jnp.einsum("thd,hde->the", query_scaled, state_in, precision=lax.Precision.HIGHEST)
    mixed = intra + inter
    power = jnp.mean(mixed * mixed, axis=-1, keepdims=True)
    normed = mixed * lax.rsqrt(power + norm_eps)
    gates = jax.nn.sigmoid(out_gate.reshape(tokens, heads_here, width).astype(jnp.float32))
    attention_out = (
        (normed * norm_gain.reshape(heads_here, width) * gates)
        .reshape(tokens, -1)
        .astype(jnp.bfloat16)
    )
    seq_count = lax.axis_size("seq")
    group = seq_count // EXP_FLY
    hits = slot_table(expert_ids, placement, CAP).reshape(EXP_FLY, CAP, tokens, 2)
    pick = jnp.sum(hits.astype(jnp.int32), axis=3).astype(jnp.bfloat16)
    share = jnp.sum(hits.astype(jnp.float32) * route_weight[None, None, :, :], axis=3)
    outgoing = jnp.einsum("jct,td->jcd", pick, features, preferred_element_type=jnp.float32).astype(
        jnp.bfloat16
    )
    fanned = jnp.broadcast_to(outgoing[:, None], (EXP_FLY, group) + outgoing.shape[1:]).reshape(
        seq_count, CAP, -1
    )
    arrived = lax.all_to_all(fanned, "seq", split_axis=0, concat_axis=0, tiled=True)
    slot_rows = arrived.reshape(seq_count * CAP, -1)
    gate = jnp.dot(slot_rows, gate_weight, preferred_element_type=jnp.float32)
    up = jnp.dot(slot_rows, up_weight, preferred_element_type=jnp.float32)
    gate_part, up_part = (
        lax.psum_scatter(gate, "head", scatter_dimension=0, tiled=True),
        lax.psum_scatter(up, "head", scatter_dimension=0, tiled=True),
    )
    hidden_part = (jax.nn.silu(gate_part) * up_part).astype(jnp.bfloat16)
    hidden = lax.all_gather(hidden_part, "head", axis=0, tiled=True)
    partial_value = jnp.dot(hidden, down_weight, preferred_element_type=jnp.float32).astype(
        jnp.bfloat16
    )
    returned = lax.all_to_all(
        partial_value.reshape(seq_count, CAP, -1), "seq", split_axis=0, concat_axis=0, tiled=True
    )
    expert_out = jnp.sum(returned.reshape(EXP_FLY, group, CAP, -1).astype(jnp.float32), axis=1)
    moe_out = jnp.einsum("jct,jcd->td", share, expert_out, precision=lax.Precision.HIGHEST).astype(
        jnp.bfloat16
    )
    return (attention_out, moe_out)


def solution(mesh):
    placed = (
        P("seq", "head"),
        P("seq", "head"),
        P("seq", "head"),
        P("seq", "head"),
        P("head", "seq"),
        P("head"),
        P("seq", "head"),
        P("seq", None),
        P("seq", None),
        P(),
        P("head", "seq"),
        P("head", "seq"),
        P("seq", "head"),
    )
    return jax.shard_map(
        per_device,
        mesh=mesh,
        in_specs=placed,
        out_specs=(P("seq", "head"), P("seq", "head")),
        check_vma=False,
    )
```

profile of v0, /device:TPU:27, one launch (start us, length us, event | category | flops | bytes accessed | tf_op | source)
XLA Modules:
  0.0 156.6 jit_solution(18189141031443075284)
XLA Ops:
  8.1 0.9 copy.88
  9.0 0.1 eq.62
  9.1 0.7 compare_convert_fusion.1
  9.8 1.2 reduce-window.16
  11.0 0.1 copy.89
  11.2 0.2 slice_reduce_fusion.1
  11.4 0.8 fusion.30
  12.2 0.2 reduce-window.19
  12.4 0.1 copy.90
  12.5 0.2 add_add_fusion
  12.6 0.1 copy.91
  12.8 1.4 convolution_convert_fusion.1
  14.2 10.9 %all_to_all.10 = bf16[8,8,1536]{2,1,0:T(8,128)(2,1)S(1)} all-to-all(bf16[8,8,1536]{2,1,0:T(8,128)(2,1)S(1)} %bitcast.102), channel_id=1, replica_groups=mesh['seq'=8,'head'=4] {'seq'}, dimensions={0} | all-to-all | bytes 393216 | tf_op jit(solution)/shard_map/all_to_all | solution.py:98
  25.1 8.6 %fusion.26 = f32[64,4608]{1,0:T(8,128)} fusion(bf16[1536,4608]{1,0:T(8,128)(2,1)} %param.25, bf16[8,8,1536]{2,1,0:T(8,128)(2,1)S(1)} %all_to_all.10), kind=kOutput, calls=%fused_computation.36 | convolution fusion | flops 905969664 | bytes 15532032 | tf_op jit(solution)/shard_map/dot_general | solution.py:100
  33.8 8.6 %fusion.24 = f32[64,4608]{1,0:T(8,128)} fusion(bf16[1536,4608]{1,0:T(8,128)(2,1)} %param.26, bf16[8,8,1536]{2,1,0:T(8,128)(2,1)S(1)} %all_to_all.10), kind=kOutput, calls=%fused_computation.34 | convolution fusion | flops 905969664 | bytes 15532032 | tf_op jit(solution)/shard_map/dot_general | solution.py:101
  42.5 0.6 reduce-window.14
  43.1 0.2 slice_reduce_fusion
  43.3 1.5 copy.94
  44.8 0.2 slice_reduce_fusion.2
  45.0 0.1 exponential_bitcast_fusion
  45.1 2.2 %fusion.5 = f32[16,128,128]{2,1,0:T(8,128)} fusion(bf16[256,16,128]{0,2,1:T(8,128)(2,1)S(1)} %bitcast.97, f32[256,16]{0,1:T(8,128)S(1)} %get-tuple-element.70, bf16[256,2048]{1,0:T(8,128)(2,1)S(1)} %copy-done.4), kind=kOutput, calls=%fused_computation.15 | convolution fusion | flops 806354944 | bytes 3162112 | tf_op jit(solution)/shard_map/thd,the->hde/dot_general | solution.py:63
  47.5 0.6 dynamic-slice
  48.7 0.2 dynamic-update-slice
  48.9 13.2 %all-reduce = f32[128]{0:T(128)S(1)} all-reduce(f32[128]{0:T(128)S(1)} %dynamic-update-slice), channel_id=2, replica_groups=mesh['seq'=8,'head'=4] {'seq'}, use_global_device_ids=true, to_apply=%add | all-reduce | flops 128 | bytes 1024
  62.1 0.1 reshape.188
  62.2 1.8 %add_divide_fusion = f32[256,2048]{1,0:T(8,128)S(1)} fusion(bf16[256,2048]{1,0:T(8,128)(2,1)} %param.18), kind=kLoop, calls=%fused_computation.10 | loop fusion | flops 2097152 | bytes 3145728 | tf_op jit(solution)/shard_map/div | solution.py:81
  64.0 1.9 %copy.87 = f32[256,2048]{0,1:T(8,128)} copy(f32[256,2048]{1,0:T(8,128)S(1)} %add_divide_fusion) | data formatting | bytes 4194304 | tf_op jit(solution)/shard_map/div | solution.py:81
  66.0 28.6 %reduce-scatter.5.cloned.1.call-done = f32[16,4608]{1,0:T(8,128)} async-done(((f32[64,4608]{1,0:T(8,128)}), f32[16,4608]{1,0:T(8,128)}) %reduce-scatter.5.cloned.1.call-update) | async-done | bytes 294928 | tf_op jit(solution)/shard_map/reduce_scatter | solution.py:104
  94.6 1.1 multiply_convert_fusion.2
  95.7 8.2 %all_gather.16 = bf16[64,4608]{1,0:T(8,128)(2,1)S(1)} all-gather(bf16[16,4608]{1,0:T(8,128)(2,1)S(1)} %multiply_convert_fusion.2), channel_id=1, replica_groups=mesh['seq'=8,'head'=4] {'head'}, dimensions={0}, use_global_device_ids=true | all-gather | bytes 737280 | tf_op jit(solution)/shard_map/all_gather | solution.py:107
  103.9 8.5 %fusion.1 = bf16[8,8,1536]{2,1,0:T(8,128)(2,1)} fusion(bf16[64,4608]{1,0:T(8,128)(2,1)S(1)} %all_gather.16, bf16[4608,1536]{1,0:T(8,128)(2,1)} %param.27), kind=kOutput, calls=%fused_computation.6 | convolution fusion | flops 906067968 | bytes 14942208 | tf_op jit(solution)/shard_map/dot_general | solution.py:108
  112.4 6.6 %all-to-all-start.1 = ((bf16[8,8,1536]{2,1,0:T(8,128)(2,1)}), bf16[8,8,1536]{2,1,0:T(8,128)(2,1)S(1)}, u32[]{:S(2)}, u32[]{:S(2)}) async-start(bf16[8,8,1536]{2,1,0:T(8,128)(2,1)} %fusion.1), calls=%async_computation.3 | async-start | bytes 393216 | tf_op jit(solution)/shard_map/all_to_all | solution.py:111
  119.0 3.0 %fusion.10 = f32[16,256,128]{1,2,0:T(8,128)} fusion(bf16[256,16,128]{0,2,1:T(8,128)(2,1)S(1)} %bitcast.98, f32[16,256]{1,0:T(8,128)S(1)} %copy_bitcast_fusion, pred[256,256]{1,0:T(8,128)(4,1)S(1)} %iota_compare_fusion, bf16[256,2048]{1,0:T(8,128)(2,1)S(1)} %copy-done.5, bf16[256,2048]{1,0:T(8,128)(2,1)S(1)} %copy-done), kind=kOutput, calls=%fused_computation.18 | convolution fusion | flops 541065216 | bytes 5324800 | tf_op jit(solution)/shard_map/hts,shd->thd/dot_general | solution.py:75
  122.0 7.8 %all-to-all-done.1 = bf16[8,8,1536]{2,1,0:T(8,128)(2,1)S(1)} async-done(((bf16[8,8,1536]{2,1,0:T(8,128)(2,1)}), bf16[8,8,1536]{2,1,0:T(8,128)(2,1)S(1)}, u32[]{:S(2)}, u32[]{:S(2)}) %all-to-all-start.1) | async-done | bytes 196640 | tf_op jit(solution)/shard_map/all_to_all | solution.py:111
  129.8 2.3 %fusion = bf16[256,1536]{1,0:T(8,128)(2,1)} fusion(f32[4,8,256]{2,1,0:T(8,128)S(1)} %select_reduce_fusion, f32[4,8,1536]{2,1,0:T(8,128)S(1)} %convert_reduce_fusion), kind=kOutput, calls=%fused_computation.4 | convolution fusion | flops 151388160 | bytes 1015808 | tf_op jit(solution)/shard_map/jct,jcd->td/dot_general | solution.py:115
  132.1 0.3 all-gather.4.cloned.1.call-done
  132.5 0.1 broadcast_in_dim.20
  132.6 10.5 %while.12 = (s32[]{:T(128)}, f32[16,128,128]{2,1,0:T(8,128)S(1)}, s32[]{:T(128)}, f32[8,16]{1,0:T(8,128)S(1)}, f32[8,16,128,128]{3,2,1,0:T(8,128)}, /*index=5*/s32[]{:T(128)}, s32[]{:T(128)}, s32[]{:T(128)}) while((s32[]{:T(128)}, f32[16,128,128]{2,1,0:T(8,128)S(1)}, s32[]{:T(128)}, f32[8,16]{1,0:T(8,128)S(1)}, f32[8,16,128,128]{3,2,1,0:T(8,128)}, ...), condition=%wide.region_3.4_spmd, body=%wide.region_2.3_spmd.sunk | while | flops 524293 | bytes 3146047 | solution.py:23
  132.6 1.4 bitcast_add_fusion.3
  134.1 1.4 bitcast_add_fusion.3
  135.6 1.4 bitcast_add_fusion.3
  137.1 1.4 bitcast_add_fusion.3
  138.6 1.4 bitcast_add_fusion.3
  140.1 1.4 bitcast_add_fusion.3
  141.6 1.4 bitcast_add_fusion.3
  143.1 4.3 %multiply_reduce_fusion = (f32[256,16]{0,1:T(8,128)S(1)}, f32[256,16,128]{0,2,1:T(8,128)S(1)}) fusion(f32[16,128,128]{2,1,0:T(8,128)S(1)} %get-tuple-element.46, f32[256,16]{0,1:T(8,128)S(1)} %get-tuple-element.69, f32[16,256,128]{1,2,0:T(8,128)} %fusion.10, bf16[256,2048]{1,0:T(8,128)(2,1)S(1)} %copy-done), kind=kOutput, calls=%fused_computation.11 | convolution fusion | flops 807923712 | bytes 6324224 | tf_op jit(solution)/shard_map/thd,hde->the/dot_general | solution.py:77
  147.4 0.4 multiply_convert_fusion.1
  147.7 1.4 copy.92
  (46 shorter events, 0.6 us)
Async XLA Ops:
  8.0 111.0 %copy-start = (bf16[256,2048]{1,0:T(8,128)(2,1)S(1)}, bf16[256,2048]{1,0:T(8,128)(2,1)}, u32[]{:S(2)}) copy-start(bf16[256,2048]{1,0:T(8,128)(2,1)} %param.15) | copy-start | bytes 3145732
  8.0 58.0 %reduce-scatter.3.cloned.1.call-start = ((), (), s32[]{:S(2)}) async-start(), calls=%async_computation.4 | async-start | bytes 1474560 | tf_op jit(solution)/shard_map/reduce_scatter | solution.py:103
  33.7 8.8 %copy-start.6 = (f32[16,256]{1,0:T(8,128)S(1)}, f32[16,256]{1,0:T(8,128)}, u32[]{:S(2)}) copy-start(f32[16,256]{1,0:T(8,128)} %param.19) | copy-start | bytes 49156
  33.7 60.9 %reduce-scatter.5.cloned.1.call-start = ((), (), s32[]{:S(2)}) async-start(), calls=%async_computation.5 | async-start | bytes 1474560 | tf_op jit(solution)/shard_map/reduce_scatter | solution.py:104
  42.4 2.7 %copy-start.4 = (bf16[256,2048]{1,0:T(8,128)(2,1)S(1)}, bf16[256,2048]{1,0:T(8,128)(2,1)}, u32[]{:S(2)}) copy-start(bf16[256,2048]{1,0:T(8,128)(2,1)} %param.17) | copy-start | bytes 3145732
  42.4 90.0 %all-gather.4.cloned.1.call-start = ((), (), s32[]{:S(2)}) async-start(), calls=%async_computation.6 | async-start | bytes 9437184 | tf_op jit(solution)/shard_map/all_gather | solution.py:15
  44.8 2.7 %copy-start.2 = (bf16[256,2048]{0,1:T(8,128)(2,1)}, bf16[256,2048]{0,1:T(8,128)(2,1)S(1)}, u32[]{:S(2)}) copy-start(bf16[256,2048]{0,1:T(8,128)(2,1)S(1)} %copy.94) | copy-start | bytes 3145732
  45.1 2.3 %copy-start.9 = (u32[32]{0:T(128)S(1)}, u32[32]{0:T(128)}, u32[]{:S(2)}) copy-start(u32[32]{0:T(128)} %constant.52) | copy-start | bytes 388
  64.0 1.9 %copy-start.8 = (f32[256,2]{0,1:T(2,128)S(1)}, f32[256,2]{0,1:T(2,128)}, u32[]{:S(2)}) copy-start(f32[256,2]{0,1:T(2,128)} %param.23) | copy-start | bytes 6148
  103.9 15.1 %copy-start.3 = (bf16[256,2048]{0,1:T(8,128)(2,1)S(1)}, bf16[256,2048]{0,1:T(8,128)(2,1)}, u32[]{:S(2)}) copy-start(bf16[256,2048]{0,1:T(8,128)(2,1)} %copy-done.2) | copy-start | bytes 3145732
  103.9 15.1 %copy-start.5 = (bf16[256,2048]{1,0:T(8,128)(2,1)S(1)}, bf16[256,2048]{1,0:T(8,128)(2,1)}, u32[]{:S(2)}) copy-start(bf16[256,2048]{1,0:T(8,128)(2,1)} %param.17) | copy-start | bytes 3145732
  112.4 17.4 %all-to-all-start.1 = ((bf16[8,8,1536]{2,1,0:T(8,128)(2,1)}), bf16[8,8,1536]{2,1,0:T(8,128)(2,1)S(1)}, u32[]{:S(2)}, u32[]{:S(2)}) async-start(bf16[8,8,1536]{2,1,0:T(8,128)(2,1)} %fusion.1), calls=%async_computation.3 | async-start | bytes 393216 | tf_op jit(solution)/shard_map/all_to_all | solution.py:111
  143.0 4.3 %copy-start.1 = (f32[256,2048]{0,1:T(8,128)S(1)}, f32[256,2048]{0,1:T(8,128)}, u32[]{:S(2)}) copy-start(f32[256,2048]{0,1:T(8,128)} %copy.87) | copy-start | bytes 6291460
  143.0 4.3 %copy-start.7 = (f32[2048]{0:T(1024)S(1)}, f32[2048]{0:T(1024)}, u32[]{:S(2)}) copy-start(f32[2048]{0:T(1024)} %param.20) | copy-start | bytes 24580
Sparse Core Ops, SparseCore 0:
  33.8 29.2 reduce-scatter.2
  66.0 28.5 reduce-scatter.4
Sparse Core Ops, SparseCore 1:
  47.5 84.9 all-gather.3
where the time goes:
time: 157 us
  matrix products  38.9 us (25%)
  waiting for transfers between devices  36.7 us (23%)
  blocking collectives  32.2 us (21%)
  other arithmetic  17.4 us (11%)
  between operations  16.4 us (10%)
  local copies, waits for them, and re-layouts  7.91 us (5%)
  starting transfers between devices  6.68 us (4%)
    reduce_scatter x1, waiting for transfers between devices, per_device(): lax.psum_scatter(up, 'head', scatter_dimension=0, tiled=True)  28.6 us
    unnamed x1, blocking collectives  13.2 us
    all_to_all x1, blocking collectives, per_device(): lax.all_to_all(fanned, 'seq', split_axis=0, concat_axis=0, tiled=True)  10.9 us
    add x7, other arithmetic, combine_states(): later[0][:, None, None] * earlier[1] + later[1]  10.1 us
    dot_general x1, matrix products, per_device(): up = jnp.dot(slot_rows, up_weight, preferred_element_type=jnp.float32)  8.61 us
    dot_general x1, matrix products, per_device(): gate = jnp.dot(slot_rows, gate_weight, preferred_element_type=jnp.float32)  8.6 us
    dot_general x1, matrix products, per_device(): jnp.dot(hidden, down_weight, preferred_element_type=jnp.float32)  8.53 us
    all_gather x1, blocking collectives, per_device(): hidden = lax.all_gather(hidden_part, 'head', axis=0, tiled=True)  8.18 us
  transfers between devices with their start and end apart: 4, of which 3 were waited for; matrix products, arithmetic and copies ran while one was open for 21% of the time, Pallas kernels for 0%

commit v1 on v0

v1 whole, which is shorter than its diff:
```python
import functools

import jax
import jax.numpy as jnp
from jax import lax
from jax.experimental import pallas as pl
from jax.experimental.pallas import tpu as pltpu
from jax.sharding import PartitionSpec as P

CAP = 8
norm_eps = 1e-06
SLOTS = 4
F32, BF16 = jnp.float32, jnp.bfloat16


def each(count, body):
    if count <= 8:
        for i in range(count):
            body(i)
    else:

        @pl.loop(0, count)
        def _(i):
            body(i)


def dot(a, b, ca=1, cb=0):
    return lax.dot_general(a, b, (((ca,), (cb,)), ((), ())), preferred_element_type=F32)


def kernel(
    cfg,
    ld, gain, ids, rw, place,
    q_hbm, k_hbm, v_hbm, g_hbm, f_hbm, wg_hbm, wu_hbm, wd_hbm,
    ao_hbm, mo_hbm,
    q, k, v, g, f, wg, wu, wd, ao, mo,
    cum, cum_t, carry, carry_in, loc, loc_in, s_in, s_out, st, intra,
    share, out_x, in_x, x, rs_out, rs_in, hid, acc, out_y, in_y,
    local_sem, weight_sem, x_send, x_recv, rs_send, rs_recv, ag_send, ag_recv,
    y_send, y_recv, chain_sem, out_sem,
):
    n_seq, n_head, experts, chunks, width, heads, hd, half = cfg
    tokens = q.shape[0]
    depth = f.shape[1]
    group = n_seq // experts
    rows = n_seq * CAP
    per = rows // n_head
    seq, head = lax.axis_index("seq"), lax.axis_index("head")
    core, chip, chips = lax.rem(seq, 2), seq // 2, n_seq // 2

    def at_seq(i):
        return {"seq": i}

    def at_head(i):
        return {"head": i}

    barrier = pltpu.get_barrier_semaphore()

    def greet_seq(r):
        pl.semaphore_signal(barrier, inc=1, device_id=at_seq(lax.rem(seq + r + 1, n_seq)),
                            device_id_type=pl.DeviceIdType.MESH)

    def greet_head(r):
        pl.semaphore_signal(barrier, inc=1, device_id=at_head(lax.rem(head + r + 1, n_head)),
                            device_id_type=pl.DeviceIdType.MESH)

    each(n_seq - 1, greet_seq)
    each(n_head - 1, greet_head)

    local = [
        pltpu.make_async_copy(a, b, local_sem.at[i])
        for i, (a, b) in enumerate(((f_hbm, f), (k_hbm, k), (v_hbm, v), (q_hbm, q), (g_hbm, g)))
    ]
    for copy in local[:3]:
        copy.start()
    up_copies, down_copies = [], []
    for c in range(chunks):
        cols = pl.ds(c * width, width)
        up_copies.append((
            pltpu.make_async_copy(wg_hbm.at[:, cols], wg.at[c], weight_sem.at[0, c]),
            pltpu.make_async_copy(wu_hbm.at[:, cols], wu.at[c], weight_sem.at[1, c]),
        ))
        down_copies.append(pltpu.make_async_copy(wd_hbm.at[cols, :], wd.at[c], weight_sem.at[2, c]))
    for a, b in up_copies:
        a.start()
        b.start()
    for copy in local[3:]:
        copy.start()
    for copy in down_copies:
        copy.start()

    t_row = lax.broadcasted_iota(jnp.int32, (tokens, tokens), 0)
    t_col = lax.broadcasted_iota(jnp.int32, (tokens, tokens), 1)
    lower = (t_row >= t_col).astype(F32).astype(BF16)
    slots = experts * CAP
    lane = lax.broadcasted_iota(jnp.int32, (tokens, slots), 1)
    wanted = jnp.full((tokens, slots), -1, jnp.int32)
    for j in range(experts):
        wanted = jnp.where(lane // CAP == j, place[j], wanted)
    first = (ids[:, 0:1] == wanted).astype(F32)
    second = (ids[:, 1:2] == wanted).astype(F32)
    match = first + second
    rank = dot(lower, match.astype(BF16))
    hit = jnp.where(rank == (lane % CAP + 1).astype(F32), match, 0.0)
    share[...] = hit * (first * rw[:, 0:1] + second * rw[:, 1:2])
    local[0].wait()
    picked = dot(hit.astype(BF16), f[...], 0, 0)
    pad = 2 * half - depth

    def pack(a):
        high = a[:, half:]
        if pad:
            high = jnp.concatenate([high, jnp.zeros((CAP, pad), F32)], axis=1)
        return jnp.concatenate([a[:, :half], high], axis=0).astype(BF16)

    for j in range(experts):
        out_x[j] = pack(picked[j * CAP:(j + 1) * CAP])
    in_x[seq] = out_x[seq // group]
    pl.semaphore_wait(barrier, n_seq - 1 + n_head - 1)

    def x_copy(r):
        to = lax.rem(seq + r + 1, n_seq)
        return pltpu.make_async_remote_copy(
            out_x.at[to // group], in_x.at[seq], x_send.at[r], x_recv.at[r],
            device_id=at_seq(to), device_id_type=pl.DeviceIdType.MESH)

    def x_arrival(r):
        src = lax.rem(seq + n_seq - r - 1, n_seq)
        return pltpu.make_async_remote_copy(
            out_x.at[0], in_x.at[src], x_send.at[r], x_recv.at[r],
            device_id=at_seq(src), device_id_type=pl.DeviceIdType.MESH)

    each(n_seq - 1, lambda r: x_copy(r).start())

    rest = ld[...]
    total, total_t = 0.0, 0.0
    for _ in range(3):
        piece = rest.astype(BF16)
        rest = rest - piece.astype(F32)
        total = total + dot(piece, lower, 1, 1)
        total_t = total_t + dot(lower, piece, 1, 1)
    cum[...] = total
    cum_t[...] = total_t
    carry[...] = jnp.broadcast_to(jnp.exp(total[:, tokens - 1:]), carry.shape)
    head_lane = lax.broadcasted_iota(jnp.int32, (tokens, heads), 1)

    def column(h):
        return jnp.sum(jnp.where(head_lane == h, cum_t[...], 0.0), axis=1, keepdims=True)

    def cols_of(h):
        return pl.ds(pl.multiple_of(h * hd, hd), hd)

    local[1].wait()
    local[2].wait()

    def own_state(h, _):
        col = column(h)
        scaled = k[:, cols_of(h)].astype(F32) * jnp.exp(col[tokens - 1:] - col)
        loc[h] = dot(scaled.astype(BF16), v[:, cols_of(h)], 0, 0).astype(BF16)
        return 0

    lax.fori_loop(0, heads, own_state, 0, unroll=True)

    def pair_copy(ref, to, n, other):
        return pltpu.make_async_remote_copy(
            ref, to, chain_sem.at[0, n], chain_sem.at[1, n],
            device_id=at_seq(other), device_id_type=pl.DeviceIdType.MESH)

    partner = seq + 1 - 2 * core
    onward = lax.rem(seq + 2, n_seq)
    loc_copy = pair_copy(loc, loc_in, 0, partner)
    carry_copy = pair_copy(carry, carry_in, 1, partner)
    state_copy = pair_copy(s_out, s_in, 2, onward)
    share_copy = pair_copy(s_in, st, 3, partner)

    @pl.when(core == 0)
    def _():
        loc_copy.start()
        carry_copy.start()

    def chain(which):
        @pl.when((core == 1) & which)
        def _():
            loc_copy.wait_recv()
            carry_copy.wait_recv()

            @pl.when(chip == 0)
            def _():
                s_in[...] = jnp.zeros_like(s_in)

            @pl.when(chip > 0)
            def _():
                state_copy.wait_recv()

            share_copy.start()

            def step(h, _):
                mid = carry_in[pl.ds(h, 1)] * s_in[h].astype(F32) + loc_in[h].astype(F32)
                st[h] = mid.astype(BF16)
                s_out[h] = (carry[pl.ds(h, 1)] * mid + loc[h].astype(F32)).astype(BF16)
                return 0

            lax.fori_loop(0, heads, step, 0)

            @pl.when(chip < chips - 1)
            def _():
                state_copy.start()

    each(n_seq - 1, lambda r: x_arrival(r).wait_recv())
    both = in_x[...].astype(F32)
    low = both[:, :CAP].reshape(rows, half)
    high = both[:, CAP:].reshape(rows, half)[:, :depth - half]
    x[...] = jnp.concatenate([low, high], axis=1).astype(BF16)
    chain(chip == 0)

    def rs_copy(c, r):
        to = lax.rem(head + r + 1, n_head)
        return pltpu.make_async_remote_copy(
            rs_out.at[c, to], rs_in.at[c, r], rs_send.at[c, r], rs_recv.at[c, r],
            device_id=at_head(to), device_id_type=pl.DeviceIdType.MESH)

    def ag_copy(c, r, src):
        to = lax.rem(head + r + 1, n_head)
        return pltpu.make_async_remote_copy(
            hid.at[c, src], hid.at[c, src], ag_send.at[c, r], ag_recv.at[c, r],
            device_id=at_head(to), device_id_type=pl.DeviceIdType.MESH)

    for c in range(chunks):
        for which, ref in enumerate((wg, wu)):
            up_copies[c][which].wait()
            part = dot(x[...], ref[c])
            rs_out[c, :, which] = part.astype(BF16).reshape(n_head, per, width)
        each(n_head - 1, lambda r, c=c: rs_copy(c, r).start())
    chain(chip == 1)

    def within(h, _):
        qh, kh, vh = (a[:, cols_of(h)] for a in (q, k, v))
        spread = column(h) - cum[pl.ds(h, 1)]
        decay = jnp.exp(jnp.where(t_row >= t_col, spread, -jnp.inf))
        probs = (dot(qh, kh, 1, 1) * decay).astype(BF16)
        intra[:, cols_of(h)] = dot(probs, vh)
        return 0

    local[3].wait()
    parts = min(chunks, heads)
    bounds = [heads * i // parts for i in range(parts + 1)]
    for c in range(chunks):
        if c < parts:
            lax.fori_loop(bounds[c], bounds[c + 1], within, 0, unroll=True)
        each(n_head - 1, lambda r, c=c: rs_copy(c, r).wait_recv())
        gate = rs_out[c, head, 0].astype(F32)
        up = rs_out[c, head, 1].astype(F32)
        for r in range(n_head - 1):
            gate += rs_in[c, r, 0].astype(F32)
            up += rs_in[c, r, 1].astype(F32)
        hid[c, head] = (gate / (1.0 + jnp.exp(-gate)) * up).astype(BF16)
        each(n_head - 1, lambda r, c=c: ag_copy(c, r, head).start())
    chain(chip == 2)

    for c in range(chunks):
        each(n_head - 1, lambda r, c=c: ag_copy(c, r, lax.rem(head + n_head - r - 1, n_head)).wait_recv())
        down_copies[c].wait()
        part = dot(hid[c].reshape(rows, width), wd[c])
        if c == 0:
            acc[...] = part
        else:
            acc[...] += part

    for b in range(n_seq):
        out_y[b] = pack(acc[b * CAP:(b + 1) * CAP, :])
    in_y[seq] = out_y[seq]

    def y_copy(r):
        to = lax.rem(seq + r + 1, n_seq)
        return pltpu.make_async_remote_copy(
            out_y.at[to], in_y.at[seq], y_send.at[r], y_recv.at[r],
            device_id=at_seq(to), device_id_type=pl.DeviceIdType.MESH)

    def y_arrival(r):
        src = lax.rem(seq + n_seq - r - 1, n_seq)
        return pltpu.make_async_remote_copy(
            out_y.at[0], in_y.at[src], y_send.at[r], y_recv.at[r],
            device_id=at_seq(src), device_id_type=pl.DeviceIdType.MESH)

    each(n_seq - 1, lambda r: y_copy(r).start())
    chain(chip >= SLOTS - 1)

    @pl.when(core == 0)
    def _():
        share_copy.wait_recv()

    local[4].wait()

    def finish(h, _):
        cols = cols_of(h)
        mixed = intra[:, cols] + jnp.exp(column(h)) * dot(q[:, cols], st[h])
        power = jnp.mean(mixed * mixed, axis=-1, keepdims=True)
        gates = 1.0 / (1.0 + jnp.exp(-g[:, cols].astype(F32)))
        ao[:, cols] = (mixed * lax.rsqrt(power + norm_eps) * gain[:, cols] * gates).astype(BF16)
        return 0

    lax.fori_loop(0, heads, finish, 0, unroll=True)
    ao_copy = pltpu.make_async_copy(ao, ao_hbm, out_sem.at[0])
    ao_copy.start()

    each(n_seq - 1, lambda r: y_arrival(r).wait_recv())
    outs = []
    for j in range(experts):
        both = in_y[j * group].astype(F32)
        for i in range(1, group):
            both += in_y[j * group + i].astype(F32)
        outs.append(jnp.concatenate([both[:CAP], both[CAP:, :depth - half]], axis=1))
    mo[...] = dot(share[...], jnp.concatenate(outs, axis=0)).astype(BF16)
    mo_copy = pltpu.make_async_copy(mo, mo_hbm, out_sem.at[1])
    mo_copy.start()

    each(n_seq - 1, lambda r: x_copy(r).wait_send())
    each(n_seq - 1, lambda r: y_copy(r).wait_send())
    for c in range(chunks):
        each(n_head - 1, lambda r, c=c: rs_copy(c, r).wait_send())
        each(n_head - 1, lambda r, c=c: ag_copy(c, r, head).wait_send())

    @pl.when(core == 0)
    def _():
        loc_copy.wait_send()
        carry_copy.wait_send()

    @pl.when(core == 1)
    def _():
        share_copy.wait_send()

        @pl.when(chip < chips - 1)
        def _():
            state_copy.wait_send()

    ao_copy.wait()
    mo_copy.wait()


def per_device(
    queries, key_input, value_input, out_gate, log_decay, norm_gain, features,
    expert_ids, route_weight, placement, gate_weight, up_weight, down_weight,
):
    n_seq, n_head = lax.axis_size("seq"), lax.axis_size("head")
    experts = placement.shape[0]
    tokens, inner = queries.shape
    heads = log_decay.shape[0]
    hd = inner // heads
    depth, hidden = gate_weight.shape
    half = -(-depth // 256) * 128
    chunks = next((n for n in (6, 4, 3, 2) if hidden % (n * 128) == 0), 1)
    width = hidden // chunks
    rows = n_seq * CAP
    per = rows // n_head
    cfg = (n_seq, n_head, experts, chunks, width, heads, hd, half)
    square = (heads, hd, hd)
    vm = pltpu.VMEM
    dma = pltpu.SemaphoreType.DMA
    vmem, anywhere = pl.BlockSpec(memory_space=pltpu.VMEM), pl.BlockSpec(memory_space=pl.ANY)
    scratch = [
        vm((tokens, inner), BF16), vm((tokens, inner), BF16), vm((tokens, inner), BF16),
        vm((tokens, inner), BF16), vm((tokens, depth), BF16),
        vm((chunks, depth, width), BF16), vm((chunks, depth, width), BF16),
        vm((chunks, width, depth), BF16), vm((tokens, inner), BF16), vm((tokens, depth), BF16),
        vm((heads, tokens), F32), vm((tokens, heads), F32), vm((heads, hd), F32), vm((heads, hd), F32),
        vm(square, BF16), vm(square, BF16), vm(square, BF16), vm(square, BF16), vm(square, BF16),
        vm((tokens, inner), F32),
        vm((tokens, experts * CAP), F32), vm((experts, 2 * CAP, half), BF16),
        vm((n_seq, 2 * CAP, half), BF16), vm((rows, depth), BF16),
        vm((chunks, n_head, 2, per, width), BF16), vm((chunks, n_head - 1, 2, per, width), BF16),
        vm((chunks, n_head, per, width), BF16), vm((rows, depth), F32),
        vm((n_seq, 2 * CAP, half), BF16), vm((n_seq, 2 * CAP, half), BF16),
        dma((5,)), dma((3, chunks)), dma((n_seq - 1,)), dma((n_seq - 1,)),
        dma((chunks, n_head - 1)), dma((chunks, n_head - 1)),
        dma((chunks, n_head - 1)), dma((chunks, n_head - 1)),
        dma((n_seq - 1,)), dma((n_seq - 1,)), dma((2, 4)), dma((2,)),
    ]
    return pl.pallas_call(
        functools.partial(kernel, cfg),
        out_shape=(
            jax.ShapeDtypeStruct((tokens, inner), BF16),
            jax.ShapeDtypeStruct((tokens, depth), BF16),
        ),
        in_specs=[vmem] * 4 + [pl.BlockSpec(memory_space=pltpu.SMEM)] + [anywhere] * 8,
        out_specs=(anywhere, anywhere),
        scratch_shapes=scratch,
        compiler_params=pltpu.CompilerParams(
            collective_id=0, has_side_effects=True, vmem_limit_bytes=60 * 1024 * 1024
        ),
    )(
        log_decay, norm_gain.reshape(1, -1), expert_ids, route_weight, placement,
        queries, key_input, value_input, out_gate, features, gate_weight, up_weight, down_weight,
    )


def solution(mesh):
    placed = (
        P("seq", "head"), P("seq", "head"), P("seq", "head"), P("seq", "head"),
        P("head", "seq"), P("head"), P("seq", "head"), P("seq", None), P("seq", None), P(),
        P("head", "seq"), P("head", "seq"), P("seq", "head"),
    )
    return jax.shard_map(
        per_device,
        mesh=mesh,
        in_specs=placed,
        out_specs=(P("seq", "head"), P("seq", "head")),
        check_vma=False,
    )
```

time: 157 us -> 58.6 us (0.37)
  the two profiles are of different devices: /device:TPU:27 before, /device:TPU:1 now
where the time goes in v1:
time: 58.6 us; the launch traced here: 58.3 us
  Pallas kernels  50.3 us (86%)
  local copies, waits for them, and re-layouts  7.32 us (12%)
  between operations  0.64 us (1%)
    pallas_call x1, Pallas kernels, per_device(): pl.pallas_call(functools.partial(kernel, cfg), out_shape=(jax.ShapeDtypeS...  50.3 us
    unnamed x4, local copies, waits for them, and re-layouts  7.32 us

profile of v1, /device:TPU:1, one launch (start us, length us, event | category | flops | bytes accessed | tf_op | source)
XLA Modules:
  0.0 58.3 jit_solution(13805529326036378738)
XLA Ops:
  0.6 1.5 %copy.15.ids = s32[256,2]{1,0:T(8,128)} copy(s32[256,2]{0,1:T(2,128)} %param.20) | data formatting | bytes 4096 | tf_op args[7]
  2.1 1.5 %copy.16.rw = f32[256,2]{1,0:T(8,128)} copy(f32[256,2]{0,1:T(2,128)} %param.21) | data formatting | bytes 4096 | tf_op args[8]
  3.6 50.3 %shard_map.140 = (bf16[256,2048]{1,0:T(8,128)(2,1)}, bf16[256,1536]{1,0:T(8,128)(2,1)}) custom-call(f32[16,256]{1,0:T(8,128)} %ld.1, f32[1,2048]{1,0:T(1,128)} %bitcast.1, s32[256,2]{1,0:T(8,128)} %copy.15.ids, f32[256,2]{1,0:T(8,128)} %copy.16.rw, s32[4]{0:T(128)} %place.1, bf16[256,2048]{1,0:T(8,128)(2,1)} %q_hbm.1, bf16[256,2048]{1,0:T(8,128)(2,1)} %k_hbm.1, ...), custom_call_target="tpu_custom_call" | custom-call | tf_op jit(solution)/shard_map/pallas_call | solution.py:378
  53.9 2.3 %copy.19 = bf16[256,2048]{1,0:T(8,128)(2,1)} copy(bf16[256,2048]{1,0:T(8,128)(2,1)} %get-tuple-element.4) | data formatting | bytes 2097152
  56.2 2.1 %copy.20 = bf16[256,1536]{1,0:T(8,128)(2,1)} copy(bf16[256,1536]{1,0:T(8,128)(2,1)} %get-tuple-element.5) | data formatting | bytes 1572864

commit v2 on v1

--- a/solution.py
+++ b/solution.py
@@ -93,18 +93,21 @@
     t_col = lax.broadcasted_iota(jnp.int32, (tokens, tokens), 1)
     lower = (t_row >= t_col).astype(F32).astype(BF16)
     slots = experts * CAP
-    lane = lax.broadcasted_iota(jnp.int32, (tokens, slots), 1)
-    wanted = jnp.full((tokens, slots), -1, jnp.int32)
+    slot = lax.broadcasted_iota(jnp.int32, (slots, tokens), 0)
+    wanted = jnp.full((slots, tokens), -1, jnp.int32)
     for j in range(experts):
-        wanted = jnp.where(lane // CAP == j, place[j], wanted)
-    first = (ids[:, 0:1] == wanted).astype(F32)
-    second = (ids[:, 1:2] == wanted).astype(F32)
+        wanted = jnp.where(slot // CAP == j, place[j], wanted)
+    first = (ids[0:1] == wanted).astype(F32)
+    second = (ids[1:2] == wanted).astype(F32)
     match = first + second
-    rank = dot(lower, match.astype(BF16))
-    hit = jnp.where(rank == (lane % CAP + 1).astype(F32), match, 0.0)
-    share[...] = hit * (first * rw[:, 0:1] + second * rw[:, 1:2])
+    rank = dot(match.astype(BF16), lower, 1, 1)
+    hit = jnp.where(rank == (slot % CAP + 1).astype(F32), match, 0.0)
+    weight = hit * (first * rw[0:1] + second * rw[1:2])
+    weight_high = weight.astype(BF16)
+    share[0:slots] = weight_high.astype(F32)
+    share[slots:] = weight - weight_high.astype(F32)
     local[0].wait()
-    picked = dot(hit.astype(BF16), f[...], 0, 0)
+    picked = dot(hit.astype(BF16), f[...])
     pad = 2 * half - depth
 
     def pack(a):
@@ -211,7 +214,6 @@
     low = both[:, :CAP].reshape(rows, half)
     high = both[:, CAP:].reshape(rows, half)[:, :depth - half]
     x[...] = jnp.concatenate([low, high], axis=1).astype(BF16)
-    chain(chip == 0)
 
     def rs_copy(c, r):
         to = lax.rem(head + r + 1, n_head)
@@ -231,7 +233,8 @@
             part = dot(x[...], ref[c])
             rs_out[c, :, which] = part.astype(BF16).reshape(n_head, per, width)
         each(n_head - 1, lambda r, c=c: rs_copy(c, r).start())
-    chain(chip == 1)
+        if c == 0:
+            chain(chip == 0)
 
     def within(h, _):
         qh, kh, vh = (a[:, cols_of(h)] for a in (q, k, v))
@@ -255,7 +258,10 @@
             up += rs_in[c, r, 1].astype(F32)
         hid[c, head] = (gate / (1.0 + jnp.exp(-gate)) * up).astype(BF16)
         each(n_head - 1, lambda r, c=c: ag_copy(c, r, head).start())
-    chain(chip == 2)
+        if c == 0:
+            chain(chip == 1)
+        if c == chunks - 1:
+            chain(chip == 2)
 
     for c in range(chunks):
         each(n_head - 1, lambda r, c=c: ag_copy(c, r, lax.rem(head + n_head - r - 1, n_head)).wait_recv())
@@ -304,13 +310,15 @@
     ao_copy.start()
 
     each(n_seq - 1, lambda r: y_arrival(r).wait_recv())
-    outs = []
-    for j in range(experts):
-        both = in_y[j * group].astype(F32)
-        for i in range(1, group):
-            both += in_y[j * group + i].astype(F32)
-        outs.append(jnp.concatenate([both[:CAP], both[CAP:, :depth - half]], axis=1))
-    mo[...] = dot(share[...], jnp.concatenate(outs, axis=0)).astype(BF16)
+    terms = []
+    for i in range(group):
+        outs = []
+        for j in range(experts):
+            both = in_y[j * group + i].astype(F32)
+            outs.append(jnp.concatenate([both[:CAP], both[CAP:, :depth - half]], axis=1))
+        terms += [jnp.concatenate(outs, axis=0).astype(BF16)] * 2
+    weights = jnp.concatenate([share[...].astype(BF16)] * group, axis=0)
+    mo[...] = dot(weights, jnp.concatenate(terms, axis=0), 0, 0).astype(BF16)
     mo_copy = pltpu.make_async_copy(mo, mo_hbm, out_sem.at[1])
     mo_copy.start()
 
@@ -365,7 +373,7 @@
         vm((heads, tokens), F32), vm((tokens, heads), F32), vm((heads, hd), F32), vm((heads, hd), F32),
         vm(square, BF16), vm(square, BF16), vm(square, BF16), vm(square, BF16), vm(square, BF16),
         vm((tokens, inner), F32),
-        vm((tokens, experts * CAP), F32), vm((experts, 2 * CAP, half), BF16),
+        vm((2 * experts * CAP, tokens), F32), vm((experts, 2 * CAP, half), BF16),
         vm((n_seq, 2 * CAP, half), BF16), vm((rows, depth), BF16),
         vm((chunks, n_head, 2, per, width), BF16), vm((chunks, n_head - 1, 2, per, width), BF16),
         vm((chunks, n_head, per, width), BF16), vm((rows, depth), F32),
@@ -375,7 +383,7 @@
         dma((chunks, n_head - 1)), dma((chunks, n_head - 1)),
         dma((n_seq - 1,)), dma((n_seq - 1,)), dma((2, 4)), dma((2,)),
     ]
-    return pl.pallas_call(
+    results = pl.pallas_call(
         functools.partial(kernel, cfg),
         out_shape=(
             jax.ShapeDtypeStruct((tokens, inner), BF16),
@@ -388,9 +396,30 @@
             collective_id=0, has_side_effects=True, vmem_limit_bytes=60 * 1024 * 1024
         ),
     )(
-        log_decay, norm_gain.reshape(1, -1), expert_ids, route_weight, placement,
+        log_decay, norm_gain.reshape(1, -1), expert_ids.T, route_weight.T, placement,
         queries, key_input, value_input, out_gate, features, gate_weight, up_weight, down_weight,
     )
+    return pl.pallas_call(
+        hand_over,
+        out_shape=tuple(jax.ShapeDtypeStruct(a.shape, a.dtype) for a in results),
+        in_specs=[anywhere] * 2,
+        out_specs=(anywhere, anywhere),
+        scratch_shapes=[dma((8,))],
+        compiler_params=pltpu.CompilerParams(vmem_limit_bytes=60 * 1024 * 1024),
+    )(*results)
+
+
+def hand_over(a, b, a_out, b_out, sem):
+    copies = []
+    for src, dst in ((a, a_out), (b, b_out)):
+        part = src.shape[0] // 4
+        for i in range(4):
+            rows = pl.ds(i * part, part)
+            copies.append(pltpu.make_async_copy(src.at[rows], dst.at[rows], sem.at[len(copies)]))
+    for copy in copies:
+        copy.start()
+    for copy in copies:
+        copy.wait()
 
 
 def solution(mesh):

time: 58.6 us -> 108 us (1.84)
  Pallas kernels: 50.3 us -> 107 us
  local copies, waits for them, and re-layouts: 7.32 us -> 0 us
    pallas_call x0 -> x1, Pallas kernels: none -> 56.8 us  [per_device(): pl.pallas_call(hand_over, out_shape=tuple((jax.ShapeDtypeStruct(a.shape,...]
    unnamed x4 -> x0, local copies, waits for them, and re-layouts: 7.32 us -> none
where the time goes in v2:
time: 108 us
  Pallas kernels  107 us (99%)
    pallas_call x1, Pallas kernels, per_device(): pl.pallas_call(hand_over, out_shape=tuple((jax.ShapeDtypeStruct(a.shape,...  56.8 us
    pallas_call x1, Pallas kernels, per_device(): pl.pallas_call(functools.partial(kernel, cfg), out_shape=(jax.ShapeDtypeS...  50.2 us

profile of v2, /device:TPU:1, one launch (start us, length us, event | category | flops | bytes accessed | tf_op | source)
XLA Modules:
  0.0 107.8 jit_solution(16761990762209943960)
XLA Ops:
  0.6 50.2 %shard_map.140 = (bf16[256,2048]{1,0:T(8,128)(2,1)}, bf16[256,1536]{1,0:T(8,128)(2,1)}) custom-call(f32[16,256]{1,0:T(8,128)} %ld.1, f32[1,2048]{1,0:T(1,128)} %bitcast.3, s32[2,256]{1,0:T(2,128)} %bitcast.4, f32[2,256]{1,0:T(2,128)} %bitcast.5, s32[4]{0:T(128)} %place.1, bf16[256,2048]{1,0:T(8,128)(2,1)} %q_hbm.1, bf16[256,2048]{1,0:T(8,128)(2,1)} %k_hbm.1, ...), custom_call_target="tpu_custom_call" | custom-call | tf_op jit(solution)/shard_map/pallas_call | solution.py:386
  50.8 56.8 %shard_map.141 = (bf16[256,2048]{1,0:T(8,128)(2,1)}, bf16[256,1536]{1,0:T(8,128)(2,1)}) custom-call(bf16[256,2048]{1,0:T(8,128)(2,1)} %get-tuple-element.4.a, bf16[256,1536]{1,0:T(8,128)(2,1)} %get-tuple-element.5.b), custom_call_target="tpu_custom_call" | custom-call | tf_op jit(solution)/shard_map/pallas_call | solution.py:402

commit v3 on v2

--- a/solution.py
+++ b/solution.py
@@ -35,7 +35,7 @@
     ao_hbm, mo_hbm,
     q, k, v, g, f, wg, wu, wd, ao, mo,
     cum, cum_t, carry, carry_in, loc, loc_in, s_in, s_out, st, intra,
-    share, out_x, in_x, x, rs_out, rs_in, hid, acc, out_y, in_y,
+    share, out_x, in_x, x, rs_out, rs_in, mid, hid, acc, out_y, in_y,
     local_sem, weight_sem, x_send, x_recv, rs_send, rs_recv, ag_send, ag_recv,
     y_send, y_recv, chain_sem, out_sem,
 ):
@@ -227,14 +227,83 @@
             hid.at[c, src], hid.at[c, src], ag_send.at[c, r], ag_recv.at[c, r],
             device_id=at_head(to), device_id_type=pl.DeviceIdType.MESH)
 
+    square = n_head == 4
+    row = head // 2
+    near = (head + 1 - 2 * (head - 2 * row), head + 2 - 4 * row)
+    far = n_head - 1 - head
+
+    def send(src, dst, sems, c, i, to):
+        return pltpu.make_async_remote_copy(
+            src, dst, sems[0].at[c, i], sems[1].at[c, i],
+            device_id=at_head(to), device_id_type=pl.DeviceIdType.MESH)
+
+    def rs_step(c, i):
+        one, two = near[c % 2], near[1 - c % 2]
+        src = (rs_out.at[c, far], rs_out.at[c, one], mid.at[c])[i]
+        return send(src, rs_in.at[c, i], (rs_send, rs_recv), c, i, two if i == 2 else one)
+
+    def ag_step(c, i):
+        block = near[c % 2] if i == 2 else head
+        to = near[1 - c % 2] if i == 2 else near[i]
+        return send(hid.at[c, block], hid.at[c, block], (ag_send, ag_recv), c, i, to)
+
+    def ag_landed(c, i):
+        block = far if i == 2 else near[i]
+        return send(hid.at[c, block], hid.at[c, block], (ag_send, ag_recv), c, i, near[0])
+
+    def reduce_start(c):
+        if square:
+            rs_step(c, 0).start()
+            rs_step(c, 1).start()
+        else:
+            each(n_head - 1, lambda r: rs_copy(c, r).start())
+
+    def reduce_middle(c):
+        if square:
+            rs_step(c, 0).wait_recv()
+            mid[c] = (rs_out[c, near[1 - c % 2]].astype(F32) + rs_in[c, 0].astype(F32)).astype(BF16)
+            rs_step(c, 2).start()
+
+    def reduce_end(c):
+        total = rs_out[c, head].astype(F32)
+        if square:
+            rs_step(c, 1).wait_recv()
+            rs_step(c, 2).wait_recv()
+            return total + rs_in[c, 1].astype(F32) + rs_in[c, 2].astype(F32)
+        each(n_head - 1, lambda r: rs_copy(c, r).wait_recv())
+        for r in range(n_head - 1):
+            total += rs_in[c, r].astype(F32)
+        return total
+
+    def gather_start(c):
+        if square:
+            ag_step(c, 0).start()
+            ag_step(c, 1).start()
+        else:
+            each(n_head - 1, lambda r: ag_copy(c, r, head).start())
+
+    def gather_middle(c):
+        if square:
+            ag_landed(c, c % 2).wait_recv()
+            ag_step(c, 2).start()
+
+    def gather_end(c):
+        if square:
+            ag_landed(c, 1 - c % 2).wait_recv()
+            ag_landed(c, 2).wait_recv()
+        else:
+            each(n_head - 1, lambda r: ag_copy(c, r, lax.rem(head + n_head - r - 1, n_head)).wait_recv())
+
     for c in range(chunks):
         for which, ref in enumerate((wg, wu)):
             up_copies[c][which].wait()
             part = dot(x[...], ref[c])
             rs_out[c, :, which] = part.astype(BF16).reshape(n_head, per, width)
-        each(n_head - 1, lambda r, c=c: rs_copy(c, r).start())
+        reduce_start(c)
         if c == 0:
             chain(chip == 0)
+        if c >= 2:
+            reduce_middle(c - 2)
 
     def within(h, _):
         qh, kh, vh = (a[:, cols_of(h)] for a in (q, k, v))
@@ -250,21 +319,23 @@
     for c in range(chunks):
         if c < parts:
             lax.fori_loop(bounds[c], bounds[c + 1], within, 0, unroll=True)
-        each(n_head - 1, lambda r, c=c: rs_copy(c, r).wait_recv())
-        gate = rs_out[c, head, 0].astype(F32)
-        up = rs_out[c, head, 1].astype(F32)
-        for r in range(n_head - 1):
-            gate += rs_in[c, r, 0].astype(F32)
-            up += rs_in[c, r, 1].astype(F32)
+        if max(0, chunks - 2) + c < chunks:
+            reduce_middle(max(0, chunks - 2) + c)
+        both = reduce_end(c)
+        gate, up = both[0], both[1]
         hid[c, head] = (gate / (1.0 + jnp.exp(-gate)) * up).astype(BF16)
-        each(n_head - 1, lambda r, c=c: ag_copy(c, r, head).start())
+        gather_start(c)
+        if c >= 1:
+            gather_middle(c - 1)
         if c == 0:
             chain(chip == 1)
         if c == chunks - 1:
             chain(chip == 2)
 
     for c in range(chunks):
-        each(n_head - 1, lambda r, c=c: ag_copy(c, r, lax.rem(head + n_head - r - 1, n_head)).wait_recv())
+        if c == 0:
+            gather_middle(chunks - 1)
+        gather_end(c)
         down_copies[c].wait()
         part = dot(hid[c].reshape(rows, width), wd[c])
         if c == 0:
@@ -325,8 +396,13 @@
     each(n_seq - 1, lambda r: x_copy(r).wait_send())
     each(n_seq - 1, lambda r: y_copy(r).wait_send())
     for c in range(chunks):
-        each(n_head - 1, lambda r, c=c: rs_copy(c, r).wait_send())
-        each(n_head - 1, lambda r, c=c: ag_copy(c, r, head).wait_send())
+        if square:
+            for i in range(n_head - 1):
+                rs_step(c, i).wait_send()
+                ag_step(c, i).wait_send()
+        else:
+            each(n_head - 1, lambda r, c=c: rs_copy(c, r).wait_send())
+            each(n_head - 1, lambda r, c=c: ag_copy(c, r, head).wait_send())
 
     @pl.when(core == 0)
     def _():
@@ -376,6 +452,7 @@
         vm((2 * experts * CAP, tokens), F32), vm((experts, 2 * CAP, half), BF16),
         vm((n_seq, 2 * CAP, half), BF16), vm((rows, depth), BF16),
         vm((chunks, n_head, 2, per, width), BF16), vm((chunks, n_head - 1, 2, per, width), BF16),
+        vm((chunks, 2, per, width), BF16),
         vm((chunks, n_head, per, width), BF16), vm((rows, depth), F32),
         vm((n_seq, 2 * CAP, half), BF16), vm((n_seq, 2 * CAP, half), BF16),
         dma((5,)), dma((3, chunks)), dma((n_seq - 1,)), dma((n_seq - 1,)),
@@ -404,22 +481,29 @@
         out_shape=tuple(jax.ShapeDtypeStruct(a.shape, a.dtype) for a in results),
         in_specs=[anywhere] * 2,
         out_specs=(anywhere, anywhere),
-        scratch_shapes=[dma((8,))],
+        scratch_shapes=[vm(a.shape, a.dtype) for a in results] + [dma((2, 4))],
         compiler_params=pltpu.CompilerParams(vmem_limit_bytes=60 * 1024 * 1024),
     )(*results)
 
 
-def hand_over(a, b, a_out, b_out, sem):
+def hand_over(a, b, a_out, b_out, a_held, b_held, sem):
     copies = []
-    for src, dst in ((a, a_out), (b, b_out)):
-        part = src.shape[0] // 4
-        for i in range(4):
+    for src, held, dst in ((b, b_held, b_out), (a, a_held, a_out)):
+        part = src.shape[0] // 2
+        for i in range(2):
             rows = pl.ds(i * part, part)
-            copies.append(pltpu.make_async_copy(src.at[rows], dst.at[rows], sem.at[len(copies)]))
-    for copy in copies:
+            n = len(copies)
+            copies.append((
+                pltpu.make_async_copy(src.at[rows], held.at[rows], sem.at[0, n]),
+                pltpu.make_async_copy(held.at[rows], dst.at[rows], sem.at[1, n]),
+            ))
+    for copy, _ in copies:
         copy.start()
-    for copy in copies:
+    for copy, on in copies:
         copy.wait()
+        on.start()
+    for _, on in copies:
+        on.wait()
 
 
 def solution(mesh):

time: 108 us -> 55.6 us (0.51)
  Pallas kernels: 107 us -> 54.3 us
    pallas_call x1, Pallas kernels: 56.8 us -> 2.32 us  [per_device(): pl.pallas_call(hand_over, out_shape=tuple((jax.ShapeDtypeStruct(a.shape,...]
    pallas_call x1, Pallas kernels: 50.2 us -> 52 us  [per_device(): pl.pallas_call(functools.partial(kernel, cfg), out_shape=(jax.ShapeDtypeS...]
where the time goes in v3:
time: 55.6 us; the launch traced here: 55.1 us
  Pallas kernels  54.3 us (98%)
  between operations  0.8 us (1%)
    pallas_call x1, Pallas kernels, per_device(): pl.pallas_call(functools.partial(kernel, cfg), out_shape=(jax.ShapeDtypeS...  52 us
    pallas_call x1, Pallas kernels, per_device(): pl.pallas_call(hand_over, out_shape=tuple((jax.ShapeDtypeStruct(a.shape,...  2.32 us

profile of v3, /device:TPU:1, one launch (start us, length us, event | category | flops | bytes accessed | tf_op | source)
XLA Modules:
  0.0 55.1 jit_solution(10672870377704915288)
XLA Ops:
  0.6 52.0 %shard_map.140 = (bf16[256,2048]{1,0:T(8,128)(2,1)}, bf16[256,1536]{1,0:T(8,128)(2,1)}) custom-call(f32[16,256]{1,0:T(8,128)} %ld.1, f32[1,2048]{1,0:T(1,128)} %bitcast.3, s32[2,256]{1,0:T(2,128)} %bitcast.4, f32[2,256]{1,0:T(2,128)} %bitcast.5, s32[4]{0:T(128)} %place.1, bf16[256,2048]{1,0:T(8,128)(2,1)} %q_hbm.1, bf16[256,2048]{1,0:T(8,128)(2,1)} %k_hbm.1, ...), custom_call_target="tpu_custom_call" | custom-call | tf_op jit(solution)/shard_map/pallas_call | solution.py:463
  52.6 2.3 %shard_map.141 = (bf16[256,2048]{1,0:T(8,128)(2,1)}, bf16[256,1536]{1,0:T(8,128)(2,1)}) custom-call(bf16[256,2048]{1,0:T(8,128)(2,1)} %get-tuple-element.4.a, bf16[256,1536]{1,0:T(8,128)(2,1)} %get-tuple-element.5.b), custom_call_target="tpu_custom_call" | custom-call | tf_op jit(solution)/shard_map/pallas_call | solution.py:479
